TPU v7x, 256 devices: a whole 4x4x8 slice. The times are simulated.
256 devices in a mesh: pipe: 4 (over x), expert: 16 (over y, z_hi), dp: 4 (over z_lo, core).
Axes of the slice: x: 4, y: 4, z: 8 (z_hi: 4, z_lo: 2; z = z_hi * 2 + z_lo), core: 2. Of those that a mesh axis runs over, the one named last changes fastest.
Arguments:
- tokens: bfloat16 [4, 2, 1024, 3584], P('pipe', None, 'expert'), may hold values from -6 to 6
- cotangent: bfloat16 [4, 2, 1024, 3584], P('pipe', None, 'expert'), may hold values from -6 to 6
- gain: float32 [4, 3584], P('pipe'), may hold values from 0.1 to 1.9
- router: bfloat16 [4, 3584, 16], P('pipe'), may hold values from -0.09375 to 0.09375
- w_gate: bfloat16 [4, 16, 3584, 1024], P('pipe', 'expert', None, 'dp'), may hold values from -0.09375 to 0.09375
- w_up: bfloat16 [4, 16, 3584, 1024], P('pipe', 'expert', None, 'dp'), may hold values from -0.09375 to 0.09375
- w_down: bfloat16 [4, 16, 1024, 3584], P('pipe', 'expert', 'dp'), may hold values from -0.1875 to 0.1875
- expert_ids: int32 [4, 2, 1024, 2], P('pipe', None, 'expert'), may hold values from 0 to 15, all different within a row; in each aligned block of 64 rows (0 to 63, 64 to 127, ..., all dimensions but the last counted through in order) at most 8 rows name the same one
Outputs:
- section_out: bfloat16 [4, 2, 1024, 3584], P('pipe', None, 'expert')
- section_grad: bfloat16 [4, 2, 1024, 3584], P('pipe', None, 'expert')
Inputs may be any that keep to these rules, and one draw needn't show every extreme that they name: `expert_ids`: in each aligned block of 64 rows (one index of expert, one layer, one micro-batch), every expert is named by exactly 8 rows.
All inputs are finite; a program needn't handle non-finite values.
Results may differ from a plain program's by a relative error of at most 0.015.
Values may be sent and summed in bfloat16 or wider, within the bound.
A program may use at most 128 MiB of HBM per device.

v0:
```python
import jax
import jax.numpy as jnp
from jax import lax
from jax.experimental import pallas as pl
from jax.experimental.pallas import tpu as pltpu
from jax.sharding import PartitionSpec as P

MESH = pl.DeviceIdType.MESH
F32 = jnp.float32
BF16 = jnp.bfloat16
HIGHEST = lax.Precision.HIGHEST

route_scale = 2.5
norm_eps = 1e-06

D = 3584
HID = 256
TOK = 128
ROWS = 256
HALF = D // 2
QUART = D // 4
CH = 256
KCH = 896


def loop(count, body):
    def step(i, carry):
        body(i)
        return carry

    lax.fori_loop(0, count, step, 0)


def dot(a, b):
    return jnp.dot(a, b, preferred_element_type=F32)


def dot_nt(a, b, precision=None):
    return lax.dot_general(
        a, b, (((1,), (1,)), ((), ())), preferred_element_type=F32, precision=precision
    )


def iota(shape, dim):
    return lax.broadcasted_iota(jnp.int32, shape, dim)


def at128(start, size):
    return pl.ds(pl.multiple_of(start, 128), size)


def at16(start, size):
    return pl.ds(pl.multiple_of(start, 16), size)


def split(value):
    high = value.astype(BF16)
    return high, (value - high.astype(F32)).astype(BF16)


def kernel(
    tok_h,
    cot_h,
    gain,
    rout_h,
    wg_h,
    wu_h,
    wd_h,
    ids,
    out_h,
    grad_h,
    hid,
    cot,
    rout,
    wg,
    wu,
    wd,
    sel,
    com,
    cwh,
    cwl,
    inv_s,
    log_s,
    send,
    full,
    act_g,
    gv,
    uv,
    act,
    gg,
    ug,
    sc,
    scs,
    scr,
    es,
    eo,
    er,
    cp,
    pa,
    pb,
    pc,
    fa,
    fb,
    fc,
    ret,
    fin,
    res,
    lsem,
    d_s,
    d_r,
    f_s,
    f_r,
    s_s,
    s_r,
    e_s,
    e_r,
    p_s,
    p_r,
    r_s,
    r_r,
    a_s,
    a_r,
    c_s,
    c_r,
    x_s,
    x_r,
    o_s,
    o_r,
    q_s,
    q_r,
):
    px = lax.axis_index("pipe")
    ex = lax.axis_index("expert")
    dx = lax.axis_index("dp")
    y = ex // 4
    zh = ex % 4
    zl = dx // 2
    c = dx % 2
    near = (zh + 2 * zl + 3) % 4
    far = (zh + 2) % 4
    opp = (zh + 5 - 2 * zl) % 4
    me = zh * 4 + y
    other = 1 - zl
    ys = [(y + dy) % 4 for dy in range(4)]
    yb = [(y + 4 - dy) % 4 for dy in range(4)]

    def dev(zh_, y_, zl_, c_):
        return (px, y_ * 4 + zh_, zl_ * 2 + c_)

    sibling = dev(zh, y, zl, 1 - c)
    partner = dev(zh, y, other, c)
    diagonal = dev(zh, y, other, 1 - c)
    after = ((px + 1) % 4, ex, dx)
    before = ((px + 3) % 4, ex, dx)

    def remote(src, dst, ssem, rsem, device):
        return pltpu.make_async_remote_copy(
            src_ref=src,
            dst_ref=dst,
            send_sem=ssem,
            recv_sem=rsem,
            device_id=device,
            device_id_type=MESH,
        )

    barrier = pltpu.get_barrier_semaphore()
    greet = [sibling, partner, diagonal, after, before]
    for dy in range(4):
        greet += [
            dev(near, ys[dy], other, c),
            dev(far, ys[dy], other, c),
            dev(near, ys[dy], zl, c),
            dev(opp, ys[dy], zl, c),
        ]
        if dy:
            greet.append(dev(zh, ys[dy], zl, c))
    for device in greet:
        pl.semaphore_signal(barrier, inc=1, device_id=device, device_id_type=MESH)

    loads = [
        pltpu.make_async_copy(a, b, lsem.at[i])
        for i, (a, b) in enumerate(
            [(cot_h, cot), (tok_h, hid), (wd_h, wd), (rout_h, rout), (wg_h, wg), (wu_h, wu)]
        )
    ]
    for load in loads:
        load.start()

    slot = iota((TOK, ROWS), 1)
    token = iota((TOK, ROWS), 0)
    slot_e = (slot // 16 % 4) * 4 + slot // 64
    first, second = ids[:, 0:1], ids[:, 1:2]
    named = ((first == slot_e) | (second == slot_e)) & (token // 64 == slot // 8 % 2)
    named = jnp.where(named, 1.0, 0.0)
    earlier = jnp.where(iota((TOK, TOK), 1) < iota((TOK, TOK), 0), 1.0, 0.0).astype(BF16)
    rank = dot(earlier, named.astype(BF16))
    picks = jnp.where(rank == (slot % 8).astype(F32), named, 0.0)
    com[...] = picks
    sel[...] = picks.T.astype(BF16)

    half = c * HALF
    loads[0].wait()

    def gather_cot(i):
        cols = at128(half + i * CH, CH)
        send[0, :, at128(i * CH, CH)] = dot(sel[...], cot[:, cols]).astype(BF16)

    loop(HALF // CH, gather_cot)
    pl.semaphore_wait(barrier, len(greet))

    mine = at16(me * 16, 16)

    def dispatch(k):
        copies = []
        for dy in range(4):
            rows = at16((near * 4 + ys[dy]) * 16, 16)
            copies.append(
                remote(
                    send.at[k, rows, :],
                    full.at[k, mine, at128(half, HALF)],
                    d_s.at[k, dy],
                    d_r.at[k, dy],
                    dev(near, ys[dy], other, c),
                )
            )
        for dy in range(4):
            rows = at16((far * 4 + ys[dy]) * 16, 16)
            copies.append(
                remote(
                    send.at[k, rows, at128(zl * QUART, QUART)],
                    full.at[k, mine, at128(half + zl * QUART, QUART)],
                    d_s.at[k, 4 + dy],
                    d_r.at[k, 4 + dy],
                    dev(far, ys[dy], other, c),
                )
            )
        for dy in range(1, 4):
            rows = at16((zh * 4 + ys[dy]) * 16, 16)
            copies.append(
                remote(
                    send.at[k, rows, :],
                    full.at[k, mine, at128(half, HALF)],
                    d_s.at[k, 7 + dy],
                    d_r.at[k, 7 + dy],
                    dev(zh, ys[dy], zl, c),
                )
            )
        for copy in copies:
            copy.start()
        full[k, mine, at128(half, HALF)] = send[k, mine, :]
        return copies

    sent = []
    sent_u = dispatch(0)

    loads[1].wait()

    def squares(i, total):
        part = hid[:, at128(i * CH, CH)].astype(F32)
        return total + part * part

    total = lax.fori_loop(0, D // CH, squares, jnp.zeros((TOK, CH), F32))
    inv = lax.rsqrt(jnp.sum(total, axis=1, keepdims=True) / D + norm_eps)
    inv_s[...] = inv

    def normed(cols):
        return (hid[:, cols].astype(F32) * inv_s[...] * gain[:, cols]).astype(BF16)

    def gather_hid(i):
        cols = at128(half + i * CH, CH)
        send[1, :, at128(i * CH, CH)] = dot(sel[...], normed(cols)).astype(BF16)

    loop(HALF // CH, gather_hid)
    sent_x = dispatch(1)

    loads[3].wait()

    def route(i, total):
        cols = at128(i * CH, CH)
        return total + dot(normed(cols), rout[cols, :])

    logits = lax.fori_loop(0, D // CH, route, jnp.zeros((TOK, 16), F32))
    log_s[...] = logits

    def chosen_parts():
        lane = iota((TOK, 16), 1)
        mask = jnp.where((ids[:, 0:1] == lane) | (ids[:, 1:2] == lane), 1.0, 0.0)
        sig = jax.nn.sigmoid(log_s[...])
        csum = jnp.sum(mask * sig, axis=1, keepdims=True)
        return mask, sig, csum, route_scale * sig * mask / csum

    spread = iota((16, ROWS), 1)
    spread = jnp.where((spread // 16 % 4) * 4 + spread // 64 == iota((16, ROWS), 0), 1.0, 0.0)
    mask, sig, csum, w16 = chosen_parts()
    w_high, w_low = split(w16)
    cwh[...] = (dot(w_high, spread.astype(BF16)) * com[...]).astype(BF16)
    cwl[...] = (dot(w_low, spread.astype(BF16)) * com[...]).astype(BF16)

    def forward(k, sent_k):
        copies = []
        for dy in range(4):
            sent_k[dy].wait_recv()
            block = full.at[k, at16((near * 4 + yb[dy]) * 16, 16), at128(half, HALF)]
            copies.append(remote(block, block, f_s.at[k, dy], f_r.at[k, dy], partner))
            copies[-1].start()
        for dy in range(4):
            sent_k[4 + dy].wait_recv()
            block = full.at[
                k,
                at16((far * 4 + yb[dy]) * 16, 16),
                at128(half + other * QUART, QUART),
            ]
            copies.append(remote(block, block, f_s.at[k, 4 + dy], f_r.at[k, 4 + dy], partner))
            copies[-1].start()
        return copies

    def to_sibling(k, place, zh_):
        block = full.at[k, at16(zh_ * 64, 64), at128(half, HALF)]
        copy = remote(block, block, s_s.at[k, place], s_r.at[k, place], sibling)
        copy.start()
        return copy

    def share_early(k, sent_k):
        for dy in range(1, 4):
            sent_k[7 + dy].wait_recv()
        return [to_sibling(k, 0, near), to_sibling(k, 1, zh)]

    def share_late(k, fwd):
        for dy in range(4):
            fwd[dy].wait_recv()
        first = to_sibling(k, 2, opp)
        for dy in range(4):
            fwd[4 + dy].wait_recv()
        return [first, to_sibling(k, 3, far)]

    fwd_u = forward(0, sent_u)
    sib = share_early(0, sent_u)
    fwd_x = forward(1, sent_x)
    sib += share_late(0, fwd_u)
    sib_x = share_early(1, sent_x)
    for copy in sib:
        copy.wait_recv()
    loads[2].wait()

    def act_grad(i, total):
        cols = at128(i * KCH, KCH)
        return total + dot_nt(full[0, :, cols], wd[:, cols])

    act_g[...] = lax.fori_loop(0, D // KCH, act_grad, jnp.zeros((ROWS, HID), F32))
    sib_x += share_late(1, fwd_x)
    loads[4].wait()
    loads[5].wait()
    for copy in sib_x:
        copy.wait_recv()
    sib += sib_x

    def expand(weight):
        def step(i, total):
            cols = at128(i * KCH, KCH)
            return total + dot(full[1, :, cols], weight[cols, :])

        return lax.fori_loop(0, D // KCH, step, jnp.zeros((ROWS, HID), F32))

    gv[...] = expand(wg)
    uv[...] = expand(wu)
    g, u, a = gv[...], uv[...], act_g[...]
    sigma = jax.nn.sigmoid(g)
    act[...] = (g * sigma * u).astype(BF16)
    gg[...] = (a * u * sigma * (1.0 + g * (1.0 - sigma))).astype(BF16)
    ug[...] = (a * g * sigma).astype(BF16)

    def down(cols):
        return dot(act[...], wd[:, cols])

    def back(cols):
        return dot_nt(gg[...], wg[cols, :]) + dot_nt(ug[...], wu[cols, :])

    theirs = (1 - c) * HALF
    swaps = []
    for k, term in ((0, down), (1, back)):

        def for_sibling(i, k=k, term=term):
            es[k, :, at128(i * CH, CH)] = term(at128(theirs + i * CH, CH)).astype(BF16)

        loop(HALF // CH, for_sibling)
        swaps.append(remote(es.at[k], er.at[k], e_s.at[k], e_r.at[k], sibling))
        swaps[-1].start()

        def for_self(i, k=k, term=term):
            eo[k, :, at128(i * CH, CH)] = term(at128(half + i * CH, CH))

        if k == 0:
            loop(HALF // CH, for_self)
            ones = jnp.ones((8, HID), F32)
            w_row = dot_nt(ones, act[...].astype(F32) * act_g[...], HIGHEST)
            n_row = dot_nt(
                ones,
                gg[...].astype(F32) * gv[...] + ug[...].astype(F32) * uv[...],
                HIGHEST,
            )
            line = iota((8, ROWS), 0)
            sc[dx] = jnp.where(line == 0, w_row, jnp.where(line == 1, n_row, 0.0))
            marks = [
                remote(sc.at[dx], sc.at[dx], a_s.at[i], a_r.at[i], device)
                for i, device in enumerate((sibling, partner, diagonal))
            ]
            for copy in marks:
                copy.start()
        else:
            last_self = for_self

    def chip_sum(k):
        swaps[k].wait_recv()

        def add(i):
            cols = at128(i * CH, CH)
            cp[k, :, cols] = (eo[k, :, cols] + er[k, :, cols].astype(F32)).astype(BF16)

        loop(HALF // CH, add)
        copies = [
            remote(cp.at[k, at16(opp * 64, 64), :], pa.at[k], p_s.at[k, 0], p_r.at[k, 0], partner),
            remote(
                cp.at[k, at16(far * 64, 64), at128(zl * QUART, QUART)],
                pb.at[k],
                p_s.at[k, 1],
                p_r.at[k, 1],
                partner,
            ),
            remote(
                cp.at[k, at16(zh * 64, 64), at128(other * QUART, QUART)],
                pc.at[k],
                p_s.at[k, 2],
                p_r.at[k, 2],
                partner,
            ),
        ]
        for copy in copies:
            copy.start()
        return copies

    pairs = [chip_sum(0)]
    loop(HALF // CH, last_self)
    pairs.append(chip_sum(1))

    for copy in marks:
        copy.wait_recv()
    scs[...] = (sc[0] + sc[1]) + (sc[2] + sc[3])
    routes_back = []
    for dy in range(4):
        routes_back += [
            (near, dy, other, 0),
            (near, dy, zl, 1),
            (far, dy, other, 2),
        ]
        if dy:
            routes_back.append((zh, dy, zl, 3))
    notes = []
    for i, (zh_, dy, zl_, kind) in enumerate(routes_back):
        notes.append(
            remote(
                scs.at[:, at128((zh_ // 2) * 128, 128)],
                scr.at[pl.ds(pl.multiple_of(me * 8, 8), 8), :],
                c_s.at[i],
                c_r.at[i],
                dev(zh_, ys[dy], zl_, c),
            )
        )
        notes[-1].start()
    scr[pl.ds(pl.multiple_of(me * 8, 8), 8), :] = scs[:, at128((zh // 2) * 128, 128)]

    def give_back(k):
        pairs[k][0].wait_recv()
        fa[k] = (cp[k, at16(near * 64, 64), :].astype(F32) + pa[k].astype(F32)).astype(BF16)
        pairs[k][1].wait_recv()
        fb[k] = (
            cp[k, at16(far * 64, 64), at128(other * QUART, QUART)].astype(F32)
            + pb[k].astype(F32)
        ).astype(BF16)
        pairs[k][2].wait_recv()
        fc[k] = (
            cp[k, at16(zh * 64, 64), at128(zl * QUART, QUART)].astype(F32) + pc[k].astype(F32)
        ).astype(BF16)
        copies = []
        for i, (zh_, dy, zl_, kind) in enumerate(routes_back):
            rows = at16(ys[dy] * 16, 16)
            if kind == 0:
                src = fa.at[k, rows, at128(other * QUART, QUART)]
            elif kind == 1:
                src = fa.at[k, rows, at128(zl * QUART, QUART)]
            elif kind == 2:
                src = fb.at[k, rows, :]
            else:
                src = fc.at[k, rows, :]
            copies.append(
                remote(
                    src,
                    ret.at[k, mine, :],
                    r_s.at[k, i],
                    r_r.at[k, i],
                    dev(zh_, ys[dy], zl_, c),
                )
            )
            copies[-1].start()
        ret[k, mine, :] = fc[k, at16(y * 16, 16), :]
        return copies

    backs = [give_back(0), give_back(1)]

    quarter = at128(half + zl * QUART, QUART)

    def combine(k):
        for copy in backs[k]:
            copy.wait_recv()
        return dot(cwh[...], ret[k]) + dot(cwl[...], ret[k])

    shifts = []

    def ship(k, device):
        shifts.append(
            remote(fin.at[k], res.at[k, :, quarter], x_s.at[k], x_r.at[k], device)
        )
        shifts[-1].start()

    fin[0] = (hid[:, quarter].astype(F32) + combine(0)).astype(BF16)
    ship(0, after)

    for copy in notes:
        copy.wait_recv()
    lane_at = (me % 8) * 16
    turn = jnp.where(iota((128, ROWS), 0) == lane_at + iota((128, ROWS), 1) % 16, 1.0, 0.0)
    moved = jnp.dot(scr[...], turn, precision=HIGHEST, preferred_element_type=F32)
    row, col = iota((128, ROWS), 0), iota((128, ROWS), 1)
    own_row = row // 8 == col // 16
    w_row = jnp.sum(jnp.where(own_row & (row % 8 == 0), moved, 0.0), axis=0, keepdims=True)
    n_row = jnp.sum(jnp.where(own_row & (row % 8 == 1), moved, 0.0), axis=0, keepdims=True)
    mask, sig, csum, w16 = chosen_parts()
    weight_grad = dot_nt(com[...] * w_row, spread, HIGHEST)
    total = jnp.sum(weight_grad * w16, axis=1, keepdims=True)
    logit_grad = (route_scale * weight_grad - total) / csum * sig * (1.0 - sig) * mask
    weighted = cwh[...].astype(F32) + cwl[...].astype(F32)
    inner = jnp.sum(weighted * n_row, axis=1, keepdims=True) + jnp.sum(
        logit_grad * log_s[...], axis=1, keepdims=True
    )
    l_high, l_low = split(logit_grad)
    inverse = inv_s[...]
    pull = inverse * inverse * inner / D

    routers = rout[quarter, :]
    normed_grad = combine(1) + (dot_nt(l_high, routers) + dot_nt(l_low, routers))
    fin[1] = (
        cot[:, quarter].astype(F32)
        + inverse * gain[:, quarter] * normed_grad
        - hid[:, quarter].astype(F32) * pull
    ).astype(BF16)
    ship(1, before)

    spreads = []
    for k in range(2):
        shifts[k].wait_recv()
        block = res.at[k, :, quarter]
        spreads.append(remote(block, block, o_s.at[k], o_r.at[k], partner))
        spreads[-1].start()
    cores = []
    for k in range(2):
        spreads[k].wait_recv()
        block = res.at[k, :, at128(half, HALF)]
        cores.append(remote(block, block, q_s.at[k], q_r.at[k], sibling))
        cores[-1].start()
    stores = []
    for k, target in ((0, out_h), (1, grad_h)):
        cores[k].wait_recv()
        stores.append(pltpu.make_async_copy(res.at[k], target, lsem.at[6 + k]))
        stores[-1].start()

    for copy in (
        sent_u
        + sent_x
        + fwd_u
        + fwd_x
        + sib
        + swaps
        + marks
        + notes
        + pairs[0]
        + pairs[1]
        + backs[0]
        + backs[1]
        + shifts
        + spreads
        + cores
    ):
        copy.wait_send()
    for copy in stores:
        copy.wait()


def shards(tokens, cotangent, gain, router, w_gate, w_up, w_down, expert_ids):
    anywhere = pl.BlockSpec(memory_space=pl.ANY)
    vmem = pl.BlockSpec(memory_space=pltpu.VMEM)

    def buf(*shape, dtype=BF16):
        return pltpu.VMEM(shape, dtype)

    def sems(*shape):
        return pltpu.SemaphoreType.DMA(shape)

    scratch = [
        buf(TOK, D),
        buf(TOK, D),
        buf(D, 16),
        buf(D, HID),
        buf(D, HID),
        buf(HID, D),
        buf(ROWS, TOK),
        buf(TOK, ROWS, dtype=F32),
        buf(TOK, ROWS),
        buf(TOK, ROWS),
        buf(TOK, 1, dtype=F32),
        buf(TOK, 16, dtype=F32),
        buf(2, ROWS, HALF),
        buf(2, ROWS, D),
        buf(ROWS, HID, dtype=F32),
        buf(ROWS, HID, dtype=F32),
        buf(ROWS, HID, dtype=F32),
        buf(ROWS, HID),
        buf(ROWS, HID),
        buf(ROWS, HID),
        buf(4, 8, ROWS, dtype=F32),
        buf(8, ROWS, dtype=F32),
        buf(128, 128, dtype=F32),
        buf(2, ROWS, HALF),
        buf(2, ROWS, HALF, dtype=F32),
        buf(2, ROWS, HALF),
        buf(2, ROWS, HALF),
        buf(2, 64, HALF),
        buf(2, 64, QUART),
        buf(2, 64, QUART),
        buf(2, 64, HALF),
        buf(2, 64, QUART),
        buf(2, 64, QUART),
        buf(2, ROWS, QUART),
        buf(2, TOK, QUART),
        buf(2, TOK, D),
        sems(8),
        sems(2, 11),
        sems(2, 11),
        sems(2, 8),
        sems(2, 8),
        sems(2, 4),
        sems(2, 4),
        sems(2),
        sems(2),
        sems(2, 3),
        sems(2, 3),
        sems(2, 15),
        sems(2, 15),
        sems(3),
        sems(3),
        sems(15),
        sems(15),
        sems(2),
        sems(2),
        sems(2),
        sems(2),
        sems(2),
        sems(2),
    ]
    out = jax.ShapeDtypeStruct((TOK, D), BF16)
    section_out, section_grad = pl.pallas_call(
        kernel,
        out_shape=(out, out),
        in_specs=[anywhere, anywhere, vmem, anywhere, anywhere, anywhere, anywhere, vmem],
        out_specs=(anywhere, anywhere),
        scratch_shapes=scratch,
        compiler_params=pltpu.CompilerParams(
            collective_id=0, has_side_effects=True, vmem_limit_bytes=56 * 1024 * 1024
        ),
    )(
        tokens.reshape(TOK, D),
        cotangent.reshape(TOK, D),
        gain,
        router.reshape(D, 16),
        w_gate.reshape(D, HID),
        w_up.reshape(D, HID),
        w_down.reshape(HID, D),
        expert_ids.reshape(TOK, 2),
    )
    return section_out.reshape(tokens.shape), section_grad.reshape(tokens.shape)


def solution(mesh):
    in_specs = (
        P("pipe", None, "expert", None),
        P("pipe", None, "expert", None),
        P("pipe", None),
        P("pipe", None, None),
        P("pipe", "expert", None, "dp"),
        P("pipe", "expert", None, "dp"),
        P("pipe", "expert", "dp", None),
        P("pipe", None, "expert", None),
    )
    out_specs = (P("pipe", None, "expert", None), P("pipe", None, "expert", None))
    return jax.shard_map(shards, mesh=mesh, in_specs=in_specs, out_specs=out_specs, check_vma=False)
```

profile of v0, /device:TPU:1, one launch (start us, length us, event | category | flops | bytes accessed | tf_op | source)
XLA Modules:
  0.0 109.3 jit_solution(1757200379511895807)
XLA Ops:
  0.6 1.4 %copy.11 = s32[1,2,64,2]{3,2,1,0:T(8,128)} copy(s32[1,2,64,2]{2,3,1,0:T(2,128)} %param.15) | data formatting | bytes 2048 | tf_op args[7]
  2.0 2.1 %copy.10 = bf16[1,3584,16]{2,1,0:T(8,128)(2,1)} copy(bf16[1,3584,16]{1,2,0:T(8,128)(2,1)} %param.11) | data formatting | bytes 229376 | tf_op args[3]
  4.2 102.0 %shard_map.95 = (bf16[128,3584]{1,0:T(8,128)(2,1)}, bf16[128,3584]{1,0:T(8,128)(2,1)}) custom-call(bf16[128,3584]{1,0:T(8,128)(2,1)} %bitcast.13, bf16[128,3584]{1,0:T(8,128)(2,1)} %bitcast.14, f32[1,3584]{1,0:T(1,128)} %gain.1, bf16[3584,16]{1,0:T(8,128)(2,1)} %bitcast.9, bf16[3584,256]{1,0:T(8,128)(2,1)} %bitcast.10, bf16[3584,256]{1,0:T(8,128)(2,1)} %bitcast.11, ...), custom_call_target="tpu_custom_call" | custom-call | tf_op jit(solution)/shard_map/pallas_call | solution.py:669
  106.1 0.0 copy-start
  106.2 2.2 %copy.14 = bf16[1,2,64,3584]{3,2,1,0:T(8,128)(2,1)} copy(bf16[1,2,64,3584]{3,2,1,0:T(8,128)(2,1)} %bitcast.16) | data formatting | bytes 1835008
  108.4 0.0 copy-done
  108.4 0.9 copy.15
Async XLA Ops:
  106.1 2.3 %copy-start = (bf16[128,3584]{1,0:T(8,128)(2,1)S(1)}, bf16[128,3584]{1,0:T(8,128)(2,1)}, u32[]{:S(2)}) copy-start(bf16[128,3584]{1,0:T(8,128)(2,1)} %get-tuple-element.5) | copy-start | bytes 2752516
where the time goes:
time: 110 us; the launch traced here: 109 us
  Pallas kernels  102 us (93%)
  local copies, waits for them, and re-layouts  6.71 us (6%)
    pallas_call x1, Pallas kernels, shards(): pl.pallas_call(kernel, out_shape=(out, out), in_specs=[anywhere, anywhere...  102 us
    unnamed x6, local copies, waits for them, and re-layouts  6.71 us

commit v1 on v0

v1 whole, which is shorter than its diff:
```python
import jax
import jax.numpy as jnp
from jax import lax
from jax.experimental import pallas as pl
from jax.experimental.pallas import tpu as pltpu
from jax.sharding import PartitionSpec as P

MESH = pl.DeviceIdType.MESH
F32 = jnp.float32
BF16 = jnp.bfloat16
HIGHEST = lax.Precision.HIGHEST

route_scale = 2.5
norm_eps = 1e-06

D = 3584
HID = 256
TOK = 128
ROWS = 256
HALF = D // 2
QUART = D // 4
PIECES = ((0, 0, 512), (0, 512, 384), (1, 0, 512), (1, 512, 384))
COUNT = len(PIECES)


def dot(a, b):
    return jnp.dot(a, b, preferred_element_type=F32)


def dot_nt(a, b, precision=None):
    return lax.dot_general(
        a, b, (((1,), (1,)), ((), ())), preferred_element_type=F32, precision=precision
    )


def iota(shape, dim):
    return lax.broadcasted_iota(jnp.int32, shape, dim)


def at128(start, size):
    return pl.ds(pl.multiple_of(start, 128), size)


def at16(start, size):
    return pl.ds(pl.multiple_of(start, 16), size)


def at8(start, size):
    return pl.ds(pl.multiple_of(start, 8), size)


def split(value):
    high = value.astype(BF16)
    return high, (value - high.astype(F32)).astype(BF16)


def kernel(
    tok_h,
    cot_h,
    gain,
    rout,
    wg_h,
    wu_h,
    wd_h,
    ids,
    out_v,
    grad_v,
    hid,
    cot,
    nrm,
    wg,
    wu,
    wd,
    sel,
    com,
    cwh,
    cwl,
    inv_s,
    log_s,
    send,
    full,
    act_g,
    gv,
    uv,
    act,
    gg,
    ug,
    sc,
    scs,
    scr,
    lsem,
    d_s,
    d_r,
    f_s,
    f_r,
    s_s,
    s_r,
    e_s,
    e_r,
    p_s,
    p_r,
    r_s,
    r_r,
    a_s,
    a_r,
    c_s,
    c_r,
    x_s,
    x_r,
    *piece_refs,
):
    bufs = [piece_refs[i * 12 : (i + 1) * 12] for i in range(COUNT)]

    px = lax.axis_index("pipe")
    ex = lax.axis_index("expert")
    dx = lax.axis_index("dp")
    y = ex // 4
    zh = ex % 4
    zl = dx // 2
    c = dx % 2
    near = (zh + 2 * zl + 3) % 4
    far = (zh + 2) % 4
    opp = (zh + 5 - 2 * zl) % 4
    me = zh * 4 + y
    other = 1 - zl
    ys = [(y + dy) % 4 for dy in range(4)]
    yb = [(y + 4 - dy) % 4 for dy in range(4)]

    def dev(zh_, y_, zl_, c_):
        return (px, y_ * 4 + zh_, zl_ * 2 + c_)

    sibling = dev(zh, y, zl, 1 - c)
    partner = dev(zh, y, other, c)
    diagonal = dev(zh, y, other, 1 - c)
    after = ((px + 1) % 4, ex, dx)
    before = ((px + 3) % 4, ex, dx)

    everything = []

    def remote(src, dst, ssem, rsem, device):
        copy = pltpu.make_async_remote_copy(
            src_ref=src,
            dst_ref=dst,
            send_sem=ssem,
            recv_sem=rsem,
            device_id=device,
            device_id_type=MESH,
        )
        copy.start()
        everything.append(copy)
        return copy

    barrier = pltpu.get_barrier_semaphore()
    greet = [sibling, partner, diagonal, after, before]
    for dy in range(4):
        greet += [
            dev(near, ys[dy], other, c),
            dev(far, ys[dy], other, c),
            dev(near, ys[dy], zl, c),
            dev(opp, ys[dy], zl, c),
        ]
        if dy:
            greet.append(dev(zh, ys[dy], zl, c))
    for device in greet:
        pl.semaphore_signal(barrier, inc=1, device_id=device, device_id_type=MESH)

    loads = [
        pltpu.make_async_copy(a, b, lsem.at[i])
        for i, (a, b) in enumerate(
            [(tok_h, hid), (cot_h, cot), (wg_h, wg), (wu_h, wu), (wd_h, wd)]
        )
    ]
    for load in loads:
        load.start()

    slot = iota((ROWS, TOK), 0)
    token = iota((ROWS, TOK), 1)
    slot_e = ((slot >> 4) & 3) * 4 + (slot >> 6)
    first = jnp.concatenate([ids[0, 0:1, :], ids[1, 0:1, :]], axis=1)
    second = jnp.concatenate([ids[0, 1:2, :], ids[1, 1:2, :]], axis=1)
    named = ((first == slot_e) | (second == slot_e)) & ((token >> 6) == ((slot >> 3) & 1))
    named = jnp.where(named, 1.0, 0.0)
    earlier = jnp.where(iota((TOK, TOK), 0) < iota((TOK, TOK), 1), 1.0, 0.0).astype(BF16)
    rank = dot(named.astype(BF16), earlier)
    picks = jnp.where(rank == (slot & 7).astype(F32), named, 0.0)
    sel[...] = picks.astype(BF16)

    half = c * HALF
    loads[0].wait()
    total = jnp.zeros((TOK, 1), F32)
    for i in range(4):
        part = hid[:, i * QUART : (i + 1) * QUART].astype(F32)
        total = total + jnp.sum(part * part, axis=1, keepdims=True)
    inv_s[...] = lax.rsqrt(total / D + norm_eps)

    def norm(start):
        for i in range(2):
            cols = at128(start + i * QUART, QUART)
            nrm[:, cols] = (hid[:, cols].astype(F32) * inv_s[...] * gain[:, cols]).astype(BF16)

    def gather(k, source):
        for i in range(2):
            send[k, :, i * QUART : (i + 1) * QUART] = dot(
                sel[...], source[:, at128(half + i * QUART, QUART)]
            ).astype(BF16)

    norm(half)
    gather(0, nrm)
    pl.semaphore_wait(barrier, len(greet))

    mine = at16(me * 16, 16)

    def dispatch(k):
        copies = []
        for dy in range(4):
            rows = at16((near * 4 + ys[dy]) * 16, 16)
            copies.append(
                remote(
                    send.at[k, rows, :],
                    full.at[k, mine, at128(half, HALF)],
                    d_s.at[k, dy],
                    d_r.at[k, dy],
                    dev(near, ys[dy], other, c),
                )
            )
        for dy in range(4):
            rows = at16((far * 4 + ys[dy]) * 16, 16)
            copies.append(
                remote(
                    send.at[k, rows, at128(zl * QUART, QUART)],
                    full.at[k, mine, at128(half + zl * QUART, QUART)],
                    d_s.at[k, 4 + dy],
                    d_r.at[k, 4 + dy],
                    dev(far, ys[dy], other, c),
                )
            )
        for dy in range(1, 4):
            rows = at16((zh * 4 + ys[dy]) * 16, 16)
            copies.append(
                remote(
                    send.at[k, rows, :],
                    full.at[k, mine, at128(half, HALF)],
                    d_s.at[k, 7 + dy],
                    d_r.at[k, 7 + dy],
                    dev(zh, ys[dy], zl, c),
                )
            )
        full[k, mine, at128(half, HALF)] = send[k, mine, :]
        return copies

    sent_x = dispatch(0)
    loads[1].wait()
    gather(1, cot)
    sent_u = dispatch(1)

    com[...] = picks.T
    norm((1 - c) * HALF)
    log_s[...] = dot_nt(nrm[...], rout[...])
    spread = iota((16, ROWS), 1)
    spread = jnp.where(
        ((spread >> 4) & 3) * 4 + (spread >> 6) == iota((16, ROWS), 0), 1.0, 0.0
    )

    def chosen_parts():
        mask = dot_nt(com[...].astype(BF16), spread.astype(BF16))
        sig = jax.nn.sigmoid(log_s[...])
        csum = jnp.sum(mask * sig, axis=1, keepdims=True)
        return mask, sig, csum, route_scale * sig * mask / csum

    mask, sig, csum, w16 = chosen_parts()
    w_high, w_low = split(w16)
    cwh[...] = (dot(w_high, spread.astype(BF16)) * com[...]).astype(BF16)
    cwl[...] = (dot(w_low, spread.astype(BF16)) * com[...]).astype(BF16)

    def forward_near(k, sent):
        copies = []
        for dy in range(4):
            sent[dy].wait_recv()
            block = full.at[k, at16((near * 4 + yb[dy]) * 16, 16), at128(half, HALF)]
            copies.append(remote(block, block, f_s.at[k, dy], f_r.at[k, dy], partner))
        return copies

    def forward_far(k, sent):
        copies = []
        for dy in range(4):
            sent[4 + dy].wait_recv()
            block = full.at[
                k,
                at16((far * 4 + yb[dy]) * 16, 16),
                at128(half + other * QUART, QUART),
            ]
            copies.append(remote(block, block, f_s.at[k, 4 + dy], f_r.at[k, 4 + dy], partner))
        return copies

    def to_sibling(k, place, zh_):
        block = full.at[k, at16(zh_ * 64, 64), at128(half, HALF)]
        return remote(block, block, s_s.at[k, place], s_r.at[k, place], sibling)

    def share_own(k, sent):
        for dy in range(1, 4):
            sent[7 + dy].wait_recv()
        return to_sibling(k, 1, zh)

    def share(k, place, zh_, copies):
        for copy in copies:
            copy.wait_recv()
        return to_sibling(k, place, zh_)

    fwd_x = forward_near(0, sent_x)
    sib_x = [to_sibling(0, 0, near)]
    fwd_x += forward_far(0, sent_x)
    sib_x.append(share_own(0, sent_x))
    sib_x.append(share(0, 2, opp, fwd_x[:4]))
    sib_x.append(share(0, 3, far, fwd_x[4:]))
    fwd_u = forward_near(1, sent_u)
    sib_u = [to_sibling(1, 0, near)]
    for load in loads[2:]:
        load.wait()
    for copy in sib_x:
        copy.wait_recv()

    gv[...] = dot(full[0], wg[...])
    uv[...] = dot(full[0], wu[...])
    g = gv[...]
    act[...] = (g * jax.nn.sigmoid(g) * uv[...]).astype(BF16)

    def down(cols):
        return dot(act[...], wd[:, cols])

    def back(cols):
        return dot_nt(gg[...], wg[cols, :]) + dot_nt(ug[...], wu[cols, :])

    terms = (down, back)
    theirs = (1 - c) * HALF

    def swap(p):
        k, off, w = PIECES[p]
        es, er = bufs[p][0], bufs[p][2]
        for i in range(2):
            es[:, i * w : (i + 1) * w] = terms[k](at128(theirs + i * QUART + off, w)).astype(BF16)
        return remote(es, er, e_s.at[p], e_r.at[p], sibling)

    def keep(p):
        k, off, w = PIECES[p]
        eo = bufs[p][1]
        for i in range(2):
            eo[:, i * w : (i + 1) * w] = terms[k](at128(half + i * QUART + off, w))

    def pair_sum(p, swapped):
        w = PIECES[p][2]
        es, eo, er, cp, pa, pb, pc = bufs[p][:7]
        swapped.wait_recv()

        def add(zh_):
            rows = at16(zh_ * 64, 64)
            cp[rows, :] = (eo[rows, :] + er[rows, :].astype(F32)).astype(BF16)
            return rows

        rows = add(far)
        copies = [
            remote(cp.at[rows, at128(zl * w, w)], pb, p_s.at[p, 0], p_r.at[p, 0], partner)
        ]
        rows = add(opp)
        copies.append(remote(cp.at[rows, :], pa, p_s.at[p, 1], p_r.at[p, 1], partner))
        rows = add(zh)
        copies.append(
            remote(cp.at[rows, at128(other * w, w)], pc, p_s.at[p, 2], p_r.at[p, 2], partner)
        )
        add(near)
        return copies

    def give_back(p, pair):
        w = PIECES[p][2]
        cp, pa, pb, pc, fa, fb, fc, ret = bufs[p][3:11]
        copies = []

        def give(src, zh_, dy, zl_):
            i = len(copies)
            copies.append(
                remote(src, ret.at[mine, :], r_s.at[p, i], r_r.at[p, i], dev(zh_, ys[dy], zl_, c))
            )

        pair[0].wait_recv()
        fb[...] = (
            cp[at16(far * 64, 64), at128(other * w, w)].astype(F32) + pb[...].astype(F32)
        ).astype(BF16)
        for dy in range(4):
            give(fb.at[at16(ys[dy] * 16, 16), :], far, dy, other)
        pair[1].wait_recv()
        fa[...] = (cp[at16(near * 64, 64), :].astype(F32) + pa[...].astype(F32)).astype(BF16)
        for dy in range(4):
            rows = at16(ys[dy] * 16, 16)
            give(fa.at[rows, at128(zl * w, w)], near, dy, zl)
            give(fa.at[rows, at128(other * w, w)], near, dy, other)
        pair[2].wait_recv()
        fc[...] = (
            cp[at16(zh * 64, 64), at128(zl * w, w)].astype(F32) + pc[...].astype(F32)
        ).astype(BF16)
        for dy in range(1, 4):
            give(fc.at[at16(ys[dy] * 16, 16), :], zh, dy, zl)
        ret[mine, :] = fc[at16(y * 16, 16), :]
        return copies

    swaps = [swap(0), swap(1)]
    keep(0)
    fwd_u += forward_far(1, sent_u)
    sib_u.append(share_own(1, sent_u))
    pairs = [pair_sum(0, swaps[0])]
    sib_u.append(share(1, 2, opp, fwd_u[:4]))
    keep(1)
    pairs.append(pair_sum(1, swaps[1]))
    sib_u.append(share(1, 3, far, fwd_u[4:]))
    for copy in sib_u:
        copy.wait_recv()

    act_g[...] = dot_nt(full[1], wd[...])
    g, u, a = gv[...], uv[...], act_g[...]
    sigma = jax.nn.sigmoid(g)
    gg[...] = (a * u * sigma * (1.0 + g * (1.0 - sigma))).astype(BF16)
    ug[...] = (a * g * sigma).astype(BF16)
    swaps += [swap(2), swap(3)]

    ones = jnp.ones((8, HID), F32)
    w_row = dot_nt(ones, act[...].astype(F32) * act_g[...], HIGHEST)
    n_row = dot_nt(
        ones, gg[...].astype(F32) * gv[...] + ug[...].astype(F32) * uv[...], HIGHEST
    )
    line = iota((8, ROWS), 0)
    sc[dx] = jnp.where(line == 0, w_row, jnp.where(line == 1, n_row, 0.0))
    marks = [
        remote(sc.at[dx], sc.at[dx], a_s.at[i], a_r.at[i], device)
        for i, device in enumerate((sibling, partner, diagonal))
    ]
    keep(2)
    backs = [give_back(0, pairs[0])]
    pairs.append(pair_sum(2, swaps[2]))
    keep(3)
    backs.append(give_back(1, pairs[1]))
    pairs.append(pair_sum(3, swaps[3]))

    for copy in marks:
        copy.wait_recv()
    scs[...] = (sc[0] + sc[1]) + (sc[2] + sc[3])
    own_notes = at8(me * 8, 8)
    notes = []
    for dy in range(4):
        for zh_, zl_ in ((near, other), (near, zl), (far, other)) + (((zh, zl),) if dy else ()):
            i = len(notes)
            notes.append(
                remote(
                    scs.at[:, at128((zh_ // 2) * 128, 128)],
                    scr.at[own_notes, :],
                    c_s.at[i],
                    c_r.at[i],
                    dev(zh_, ys[dy], zl_, c),
                )
            )
    scr[own_notes, :] = scs[:, at128((zh // 2) * 128, 128)]

    quarter = half + zl * QUART
    results = (out_v, grad_v)

    def combine(p):
        ret = bufs[p][10]
        for copy in backs[p]:
            copy.wait_recv()
        return dot(cwh[...], ret[...]) + dot(cwl[...], ret[...])

    def ship(p, value, device):
        k, off, w = PIECES[p]
        fin = bufs[p][11]
        fin[...] = value.astype(BF16)
        return remote(
            fin, results[k].at[:, at128(quarter + off, w)], x_s.at[p, 0], x_r.at[p, 0], device
        )

    def pass_on(p, shift):
        k, off, w = PIECES[p]
        shift.wait_recv()
        block = results[k].at[:, at128(quarter + off, w)]
        return [
            remote(block, block, x_s.at[p, 1], x_r.at[p, 1], partner),
            remote(block, block, x_s.at[p, 2], x_r.at[p, 2], sibling),
        ]

    def pass_last(p, passed):
        k, off, w = PIECES[p]
        passed[0].wait_recv()
        block = results[k].at[:, at128(half + other * QUART + off, w)]
        passed.append(remote(block, block, x_s.at[p, 3], x_r.at[p, 3], sibling))

    shifts = []
    for p in range(2):
        k, off, w = PIECES[p]
        shifts.append(
            ship(p, hid[:, at128(quarter + off, w)].astype(F32) + combine(p), after)
        )
    backs.append(give_back(2, pairs[2]))
    passed = [pass_on(0, shifts[0])]
    backs.append(give_back(3, pairs[3]))
    passed.append(pass_on(1, shifts[1]))

    for copy in notes:
        copy.wait_recv()
    lane_at = (me % 8) * 16
    row, col = iota((128, ROWS), 0), iota((128, ROWS), 1)
    turn = jnp.where(row == lane_at + (col & 15), 1.0, 0.0)
    moved = jnp.dot(scr[...], turn, precision=HIGHEST, preferred_element_type=F32)
    own_row = (row >> 3) == (col >> 4)
    w_row = jnp.sum(jnp.where(own_row & ((row & 7) == 0), moved, 0.0), axis=0, keepdims=True)
    n_row = jnp.sum(jnp.where(own_row & ((row & 7) == 1), moved, 0.0), axis=0, keepdims=True)
    mask, sig, csum, w16 = chosen_parts()
    weight_grad = dot_nt(com[...] * w_row, spread, HIGHEST)
    total = jnp.sum(weight_grad * w16, axis=1, keepdims=True)
    logit_grad = (route_scale * weight_grad - total) / csum * sig * (1.0 - sig) * mask
    weighted = cwh[...].astype(F32) + cwl[...].astype(F32)
    inner = jnp.sum(weighted * n_row, axis=1, keepdims=True) + jnp.sum(
        logit_grad * log_s[...], axis=1, keepdims=True
    )
    l_high, l_low = split(logit_grad)
    inverse = inv_s[...]
    pull = inverse * inverse * inner / D

    def gradient(p):
        k, off, w = PIECES[p]
        cols = at128(quarter + off, w)
        routers = rout[:, cols]
        normed_grad = combine(p) + (dot(l_high, routers) + dot(l_low, routers))
        return (
            cot[:, cols].astype(F32)
            + inverse * gain[:, cols] * normed_grad
            - hid[:, cols].astype(F32) * pull
        )

    shifts.append(ship(2, gradient(2), before))
    pass_last(0, passed[0])
    pass_last(1, passed[1])
    shifts.append(ship(3, gradient(3), before))
    passed.append(pass_on(2, shifts[2]))
    passed.append(pass_on(3, shifts[3]))
    pass_last(2, passed[2])
    pass_last(3, passed[3])
    for copies in passed:
        copies[1].wait_recv()
        copies[2].wait_recv()
    for copy in everything:
        copy.wait_send()


def shards(tokens, cotangent, gain, router, w_gate, w_up, w_down, expert_ids):
    anywhere = pl.BlockSpec(memory_space=pl.ANY)
    vmem = pl.BlockSpec(memory_space=pltpu.VMEM)

    def buf(*shape, dtype=BF16):
        return pltpu.VMEM(shape, dtype)

    def sems(*shape):
        return pltpu.SemaphoreType.DMA(shape)

    scratch = [
        buf(TOK, D),
        buf(TOK, D),
        buf(TOK, D),
        buf(D, HID),
        buf(D, HID),
        buf(HID, D),
        buf(ROWS, TOK),
        buf(TOK, ROWS, dtype=F32),
        buf(TOK, ROWS),
        buf(TOK, ROWS),
        buf(TOK, 1, dtype=F32),
        buf(TOK, 16, dtype=F32),
        buf(2, ROWS, HALF),
        buf(2, ROWS, D),
        buf(ROWS, HID, dtype=F32),
        buf(ROWS, HID, dtype=F32),
        buf(ROWS, HID, dtype=F32),
        buf(ROWS, HID),
        buf(ROWS, HID),
        buf(ROWS, HID),
        buf(4, 8, ROWS, dtype=F32),
        buf(8, ROWS, dtype=F32),
        buf(128, 128, dtype=F32),
        sems(5),
        sems(2, 11),
        sems(2, 11),
        sems(2, 8),
        sems(2, 8),
        sems(2, 4),
        sems(2, 4),
        sems(COUNT),
        sems(COUNT),
        sems(COUNT, 3),
        sems(COUNT, 3),
        sems(COUNT, 15),
        sems(COUNT, 15),
        sems(3),
        sems(3),
        sems(15),
        sems(15),
        sems(COUNT, 4),
        sems(COUNT, 4),
    ]
    for _, _, w in PIECES:
        scratch += [
            buf(ROWS, 2 * w),
            buf(ROWS, 2 * w, dtype=F32),
            buf(ROWS, 2 * w),
            buf(ROWS, 2 * w),
            buf(64, 2 * w),
            buf(64, w),
            buf(64, w),
            buf(64, 2 * w),
            buf(64, w),
            buf(64, w),
            buf(ROWS, w),
            buf(TOK, w),
        ]
    out = pltpu.VMEM((TOK, D), BF16)
    section_out, section_grad = pl.pallas_call(
        kernel,
        out_shape=(out, out),
        in_specs=[anywhere, anywhere, vmem, vmem, anywhere, anywhere, anywhere, vmem],
        out_specs=(vmem, vmem),
        scratch_shapes=scratch,
        compiler_params=pltpu.CompilerParams(
            collective_id=0, has_side_effects=True, vmem_limit_bytes=56 * 1024 * 1024
        ),
    )(
        tokens.reshape(TOK, D),
        cotangent.reshape(TOK, D),
        gain,
        jnp.swapaxes(router.reshape(D, 16), 0, 1),
        w_gate.reshape(D, HID),
        w_up.reshape(D, HID),
        w_down.reshape(HID, D),
        jnp.swapaxes(expert_ids.reshape(2, TOK // 2, 2), 1, 2),
    )
    return section_out.reshape(tokens.shape), section_grad.reshape(tokens.shape)


def solution(mesh):
    in_specs = (
        P("pipe", None, "expert", None),
        P("pipe", None, "expert", None),
        P("pipe", None),
        P("pipe", None, None),
        P("pipe", "expert", None, "dp"),
        P("pipe", "expert", None, "dp"),
        P("pipe", "expert", "dp", None),
        P("pipe", None, "expert", None),
    )
    out_specs = (P("pipe", None, "expert", None), P("pipe", None, "expert", None))
    return jax.shard_map(shards, mesh=mesh, in_specs=in_specs, out_specs=out_specs, check_vma=False)
```

time: 110 us -> 87.5 us (0.80)
  Pallas kernels: 102 us -> 84.9 us
  local copies, waits for them, and re-layouts: 6.71 us -> 1.85 us
    pallas_call x1, Pallas kernels: 102 us -> 84.9 us  [shards(): pl.pallas_call(kernel, out_shape=(out, out), in_specs=[anywhere, anywhere...]
    unnamed x6 -> x2, local copies, waits for them, and re-layouts: 6.71 us -> 1.85 us
where the time goes in v1:
time: 87.5 us; the launch traced here: 87.4 us
  Pallas kernels  84.9 us (97%)
  local copies, waits for them, and re-layouts  1.85 us (2%)
    pallas_call x1, Pallas kernels, shards(): pl.pallas_call(kernel, out_shape=(out, out), in_specs=[anywhere, anywhere...  84.9 us
    unnamed x2, local copies, waits for them, and re-layouts  1.85 us

profile of v1, /device:TPU:1, one launch (start us, length us, event | category | flops | bytes accessed | tf_op | source)
XLA Modules:
  0.0 87.4 jit_solution(8602589256290913884)
XLA Ops:
  0.6 84.9 %shard_map.95 = (bf16[128,3584]{1,0:T(8,128)(2,1)S(1)}, bf16[128,3584]{1,0:T(8,128)(2,1)S(1)}) custom-call(bf16[128,3584]{1,0:T(8,128)(2,1)} %bitcast.18, bf16[128,3584]{1,0:T(8,128)(2,1)} %bitcast.19, f32[1,3584]{1,0:T(1,128)} %gain.1, bf16[16,3584]{1,0:T(8,128)(2,1)} %bitcast.20, bf16[3584,256]{1,0:T(8,128)(2,1)} %bitcast.15, bf16[3584,256]{1,0:T(8,128)(2,1)} %bitcast.16, ...), custom_call_target="tpu_custom_call" | custom-call | tf_op jit(solution)/shard_map/pallas_call | solution.py:620
  85.5 0.9 %copy.12 = bf16[1,2,64,3584]{3,2,1,0:T(8,128)(2,1)} copy(bf16[1,2,64,3584]{3,2,1,0:T(8,128)(2,1)S(1)} %bitcast.14) | data formatting | bytes 1835008
  86.5 0.9 %copy.13 = bf16[1,2,64,3584]{3,2,1,0:T(8,128)(2,1)} copy(bf16[1,2,64,3584]{3,2,1,0:T(8,128)(2,1)S(1)} %bitcast.13) | data formatting | bytes 1835008

commit v2 on v1

--- a/solution.py
+++ b/solution.py
@@ -57,14 +57,17 @@
 def kernel(
     tok_h,
     cot_h,
-    gain,
-    rout,
+    gain_h,
+    rout_h,
     wg_h,
     wu_h,
     wd_h,
-    ids,
+    ids_h,
     out_v,
     grad_v,
+    ids,
+    gain,
+    rout,
     hid,
     cot,
     nrm,
@@ -135,8 +138,6 @@
     after = ((px + 1) % 4, ex, dx)
     before = ((px + 3) % 4, ex, dx)
 
-    everything = []
-
     def remote(src, dst, ssem, rsem, device):
         copy = pltpu.make_async_remote_copy(
             src_ref=src,
@@ -147,31 +148,34 @@
             device_id_type=MESH,
         )
         copy.start()
-        everything.append(copy)
         return copy
 
+    def take(ref, sem):
+        pltpu.make_async_copy(ref, ref, sem).wait()
+
     barrier = pltpu.get_barrier_semaphore()
-    greet = [sibling, partner, diagonal, after, before]
-    for dy in range(4):
+    greet = []
+    for dy in (2, 1, 3, 0):
         greet += [
-            dev(near, ys[dy], other, c),
             dev(far, ys[dy], other, c),
             dev(near, ys[dy], zl, c),
             dev(opp, ys[dy], zl, c),
+            dev(near, ys[dy], other, c),
         ]
         if dy:
             greet.append(dev(zh, ys[dy], zl, c))
+    greet += [after, before, partner, diagonal, sibling]
     for device in greet:
         pl.semaphore_signal(barrier, inc=1, device_id=device, device_id_type=MESH)
 
+    names = (ids, hid, gain, cot, wg, wu, wd, rout)
+    sources = (ids_h, tok_h, gain_h, cot_h, wg_h, wu_h, wd_h, rout_h)
     loads = [
-        pltpu.make_async_copy(a, b, lsem.at[i])
-        for i, (a, b) in enumerate(
-            [(tok_h, hid), (cot_h, cot), (wg_h, wg), (wu_h, wu), (wd_h, wd)]
-        )
+        pltpu.make_async_copy(a, b, lsem.at[i]) for i, (a, b) in enumerate(zip(sources, names))
     ]
-    for load in loads:
+    for load in loads[:3]:
         load.start()
+    loads[0].wait()
 
     slot = iota((ROWS, TOK), 0)
     token = iota((ROWS, TOK), 1)
@@ -186,7 +190,9 @@
     sel[...] = picks.astype(BF16)
 
     half = c * HALF
-    loads[0].wait()
+    loads[1].wait()
+    for load in loads[3:]:
+        load.start()
     total = jnp.zeros((TOK, 1), F32)
     for i in range(4):
         part = hid[:, i * QUART : (i + 1) * QUART].astype(F32)
@@ -204,84 +210,58 @@
                 sel[...], source[:, at128(half + i * QUART, QUART)]
             ).astype(BF16)
 
+    loads[2].wait()
     norm(half)
     gather(0, nrm)
     pl.semaphore_wait(barrier, len(greet))
 
     mine = at16(me * 16, 16)
 
-    def dispatch(k):
-        copies = []
-        for dy in range(4):
-            rows = at16((near * 4 + ys[dy]) * 16, 16)
-            copies.append(
-                remote(
-                    send.at[k, rows, :],
-                    full.at[k, mine, at128(half, HALF)],
-                    d_s.at[k, dy],
-                    d_r.at[k, dy],
-                    dev(near, ys[dy], other, c),
-                )
-            )
-        for dy in range(4):
-            rows = at16((far * 4 + ys[dy]) * 16, 16)
-            copies.append(
-                remote(
-                    send.at[k, rows, at128(zl * QUART, QUART)],
-                    full.at[k, mine, at128(half + zl * QUART, QUART)],
-                    d_s.at[k, 4 + dy],
-                    d_r.at[k, 4 + dy],
-                    dev(far, ys[dy], other, c),
-                )
-            )
-        for dy in range(1, 4):
-            rows = at16((zh * 4 + ys[dy]) * 16, 16)
-            copies.append(
-                remote(
-                    send.at[k, rows, :],
-                    full.at[k, mine, at128(half, HALF)],
-                    d_s.at[k, 7 + dy],
-                    d_r.at[k, 7 + dy],
-                    dev(zh, ys[dy], zl, c),
-                )
-            )
-        full[k, mine, at128(half, HALF)] = send[k, mine, :]
-        return copies
-
-    sent_x = dispatch(0)
-    loads[1].wait()
+    def send_near(k, dy):
+        rows = at16((near * 4 + ys[dy]) * 16, 16)
+        return remote(
+            send.at[k, rows, :],
+            full.at[k, mine, at128(half, HALF)],
+            d_s.at[k],
+            d_r.at[k, dy],
+            dev(near, ys[dy], other, c),
+        )
+
+    def send_far(k, dy):
+        rows = at16((far * 4 + ys[dy]) * 16, 16)
+        return remote(
+            send.at[k, rows, at128(zl * QUART, QUART)],
+            full.at[k, mine, at128(half + zl * QUART, QUART)],
+            d_s.at[k],
+            d_r.at[k, 4 + dy],
+            dev(far, ys[dy], other, c),
+        )
+
+    def send_own(k, dy):
+        rows = at16((zh * 4 + ys[dy]) * 16, 16)
+        return remote(
+            send.at[k, rows, :],
+            full.at[k, mine, at128(half, HALF)],
+            d_s.at[k],
+            d_r.at[k, 8],
+            dev(zh, ys[dy], zl, c),
+        )
+
+    sent_x = [send_near(0, dy) for dy in range(4)]
+    sent_x += [send_far(0, dy) for dy in range(4)]
+    sent_x += [send_own(0, dy) for dy in range(1, 4)]
+    full[0, mine, at128(half, HALF)] = send[0, mine, :]
+    loads[3].wait()
     gather(1, cot)
-    sent_u = dispatch(1)
-
-    com[...] = picks.T
-    norm((1 - c) * HALF)
-    log_s[...] = dot_nt(nrm[...], rout[...])
-    spread = iota((16, ROWS), 1)
-    spread = jnp.where(
-        ((spread >> 4) & 3) * 4 + (spread >> 6) == iota((16, ROWS), 0), 1.0, 0.0
-    )
-
-    def chosen_parts():
-        mask = dot_nt(com[...].astype(BF16), spread.astype(BF16))
-        sig = jax.nn.sigmoid(log_s[...])
-        csum = jnp.sum(mask * sig, axis=1, keepdims=True)
-        return mask, sig, csum, route_scale * sig * mask / csum
-
-    mask, sig, csum, w16 = chosen_parts()
-    w_high, w_low = split(w16)
-    cwh[...] = (dot(w_high, spread.astype(BF16)) * com[...]).astype(BF16)
-    cwl[...] = (dot(w_low, spread.astype(BF16)) * com[...]).astype(BF16)
+    full[1, mine, at128(half, HALF)] = send[1, mine, :]
 
     def forward_near(k, sent):
-        copies = []
         for dy in range(4):
             sent[dy].wait_recv()
             block = full.at[k, at16((near * 4 + yb[dy]) * 16, 16), at128(half, HALF)]
-            copies.append(remote(block, block, f_s.at[k, dy], f_r.at[k, dy], partner))
-        return copies
+            remote(block, block, f_s.at[k], f_r.at[k, 0], partner)
 
     def forward_far(k, sent):
-        copies = []
         for dy in range(4):
             sent[4 + dy].wait_recv()
             block = full.at[
@@ -289,35 +269,64 @@
                 at16((far * 4 + yb[dy]) * 16, 16),
                 at128(half + other * QUART, QUART),
             ]
-            copies.append(remote(block, block, f_s.at[k, 4 + dy], f_r.at[k, 4 + dy], partner))
-        return copies
-
-    def to_sibling(k, place, zh_):
+            remote(block, block, f_s.at[k], f_r.at[k, 1], partner)
+
+    def to_sibling(k, zh_):
         block = full.at[k, at16(zh_ * 64, 64), at128(half, HALF)]
-        return remote(block, block, s_s.at[k, place], s_r.at[k, place], sibling)
-
-    def share_own(k, sent):
-        for dy in range(1, 4):
-            sent[7 + dy].wait_recv()
-        return to_sibling(k, 1, zh)
-
-    def share(k, place, zh_, copies):
-        for copy in copies:
-            copy.wait_recv()
-        return to_sibling(k, place, zh_)
-
-    fwd_x = forward_near(0, sent_x)
-    sib_x = [to_sibling(0, 0, near)]
-    fwd_x += forward_far(0, sent_x)
-    sib_x.append(share_own(0, sent_x))
-    sib_x.append(share(0, 2, opp, fwd_x[:4]))
-    sib_x.append(share(0, 3, far, fwd_x[4:]))
-    fwd_u = forward_near(1, sent_u)
-    sib_u = [to_sibling(1, 0, near)]
-    for load in loads[2:]:
+        remote(block, block, s_s.at[k], s_r.at[k], sibling)
+
+    def share_own(k):
+        take(full.at[k, at16(zh * 64, 48), at128(half, HALF)], d_r.at[k, 8])
+        to_sibling(k, zh)
+
+    def share_opp(k):
+        take(full.at[k, at16(opp * 64, 64), at128(half, HALF)], f_r.at[k, 0])
+        to_sibling(k, opp)
+
+    def share_far(k):
+        take(full.at[k, at16(far * 64, 64), at128(half + zl * QUART, QUART)], f_r.at[k, 1])
+        to_sibling(k, far)
+
+    theirs = (1 - c) * HALF
+
+    def complete(k):
+        take(full.at[k, :, at128(theirs, HALF)], s_r.at[k])
+
+    sent_u = [send_near(1, dy) for dy in range(4)]
+    sent_u += [send_far(1, dy) for dy in range(4)]
+    sent_u += [send_own(1, dy) for dy in range(1, 4)]
+    forward_near(0, sent_x)
+    to_sibling(0, near)
+    forward_far(0, sent_x)
+    share_own(0)
+
+    com[...] = picks.T
+    loads[7].wait()
+    norm((1 - c) * HALF)
+    log_s[...] = dot_nt(nrm[...], rout[...])
+    spread = iota((16, ROWS), 1)
+    spread = jnp.where(
+        ((spread >> 4) & 3) * 4 + (spread >> 6) == iota((16, ROWS), 0), 1.0, 0.0
+    )
+
+    def chosen_parts():
+        mask = dot_nt(com[...].astype(BF16), spread.astype(BF16))
+        sig = jax.nn.sigmoid(log_s[...])
+        csum = jnp.sum(mask * sig, axis=1, keepdims=True)
+        return mask, sig, csum, route_scale * sig * mask / csum
+
+    mask, sig, csum, w16 = chosen_parts()
+    w_high, w_low = split(w16)
+    cwh[...] = (dot(w_high, spread.astype(BF16)) * com[...]).astype(BF16)
+    cwl[...] = (dot(w_low, spread.astype(BF16)) * com[...]).astype(BF16)
+
+    share_opp(0)
+    share_far(0)
+    forward_near(1, sent_u)
+    to_sibling(1, near)
+    for load in loads[4:7]:
         load.wait()
-    for copy in sib_x:
-        copy.wait_recv()
+    complete(0)
 
     gv[...] = dot(full[0], wg[...])
     uv[...] = dot(full[0], wu[...])
@@ -331,8 +340,6 @@
         return dot_nt(gg[...], wg[cols, :]) + dot_nt(ug[...], wu[cols, :])
 
     terms = (down, back)
-    theirs = (1 - c) * HALF
-
     def swap(p):
         k, off, w = PIECES[p]
         es, er = bufs[p][0], bufs[p][2]
@@ -358,13 +365,13 @@
 
         rows = add(far)
         copies = [
-            remote(cp.at[rows, at128(zl * w, w)], pb, p_s.at[p, 0], p_r.at[p, 0], partner)
+            remote(cp.at[rows, at128(zl * w, w)], pb, p_s.at[p], p_r.at[p, 0], partner)
         ]
         rows = add(opp)
-        copies.append(remote(cp.at[rows, :], pa, p_s.at[p, 1], p_r.at[p, 1], partner))
+        copies.append(remote(cp.at[rows, :], pa, p_s.at[p], p_r.at[p, 1], partner))
         rows = add(zh)
         copies.append(
-            remote(cp.at[rows, at128(other * w, w)], pc, p_s.at[p, 2], p_r.at[p, 2], partner)
+            remote(cp.at[rows, at128(other * w, w)], pc, p_s.at[p], p_r.at[p, 2], partner)
         )
         add(near)
         return copies
@@ -372,13 +379,9 @@
     def give_back(p, pair):
         w = PIECES[p][2]
         cp, pa, pb, pc, fa, fb, fc, ret = bufs[p][3:11]
-        copies = []
 
         def give(src, zh_, dy, zl_):
-            i = len(copies)
-            copies.append(
-                remote(src, ret.at[mine, :], r_s.at[p, i], r_r.at[p, i], dev(zh_, ys[dy], zl_, c))
-            )
+            remote(src, ret.at[mine, :], r_s.at[p], r_r.at[p], dev(zh_, ys[dy], zl_, c))
 
         pair[0].wait_recv()
         fb[...] = (
@@ -399,19 +402,17 @@
         for dy in range(1, 4):
             give(fc.at[at16(ys[dy] * 16, 16), :], zh, dy, zl)
         ret[mine, :] = fc[at16(y * 16, 16), :]
-        return copies
 
     swaps = [swap(0), swap(1)]
     keep(0)
-    fwd_u += forward_far(1, sent_u)
-    sib_u.append(share_own(1, sent_u))
+    forward_far(1, sent_u)
+    share_own(1)
     pairs = [pair_sum(0, swaps[0])]
-    sib_u.append(share(1, 2, opp, fwd_u[:4]))
+    share_opp(1)
     keep(1)
     pairs.append(pair_sum(1, swaps[1]))
-    sib_u.append(share(1, 3, far, fwd_u[4:]))
-    for copy in sib_u:
-        copy.wait_recv()
+    share_far(1)
+    complete(1)
 
     act_g[...] = dot_nt(full[1], wd[...])
     g, u, a = gv[...], uv[...], act_g[...]
@@ -427,33 +428,26 @@
     )
     line = iota((8, ROWS), 0)
     sc[dx] = jnp.where(line == 0, w_row, jnp.where(line == 1, n_row, 0.0))
-    marks = [
-        remote(sc.at[dx], sc.at[dx], a_s.at[i], a_r.at[i], device)
-        for i, device in enumerate((sibling, partner, diagonal))
-    ]
+    for device in (sibling, partner, diagonal):
+        remote(sc.at[dx], sc.at[dx], a_s.at[0], a_r.at[0], device)
     keep(2)
-    backs = [give_back(0, pairs[0])]
+    give_back(0, pairs[0])
     pairs.append(pair_sum(2, swaps[2]))
     keep(3)
-    backs.append(give_back(1, pairs[1]))
+    give_back(1, pairs[1])
     pairs.append(pair_sum(3, swaps[3]))
 
-    for copy in marks:
-        copy.wait_recv()
+    take(sc.at[0:3], a_r.at[0])
     scs[...] = (sc[0] + sc[1]) + (sc[2] + sc[3])
     own_notes = at8(me * 8, 8)
-    notes = []
     for dy in range(4):
         for zh_, zl_ in ((near, other), (near, zl), (far, other)) + (((zh, zl),) if dy else ()):
-            i = len(notes)
-            notes.append(
-                remote(
-                    scs.at[:, at128((zh_ // 2) * 128, 128)],
-                    scr.at[own_notes, :],
-                    c_s.at[i],
-                    c_r.at[i],
-                    dev(zh_, ys[dy], zl_, c),
-                )
+            remote(
+                scs.at[:, at128((zh_ // 2) * 128, 128)],
+                scr.at[own_notes, :],
+                c_s.at[0],
+                c_r.at[0],
+                dev(zh_, ys[dy], zl_, c),
             )
     scr[own_notes, :] = scs[:, at128((zh // 2) * 128, 128)]
 
@@ -462,8 +456,7 @@
 
     def combine(p):
         ret = bufs[p][10]
-        for copy in backs[p]:
-            copy.wait_recv()
+        take(ret.at[0:240, :], r_r.at[p])
         return dot(cwh[...], ret[...]) + dot(cwl[...], ret[...])
 
     def ship(p, value, device):
@@ -471,37 +464,34 @@
         fin = bufs[p][11]
         fin[...] = value.astype(BF16)
         return remote(
-            fin, results[k].at[:, at128(quarter + off, w)], x_s.at[p, 0], x_r.at[p, 0], device
+            fin, results[k].at[:, at128(quarter + off, w)], x_s.at[p], x_r.at[p, 0], device
         )
 
     def pass_on(p, shift):
         k, off, w = PIECES[p]
         shift.wait_recv()
         block = results[k].at[:, at128(quarter + off, w)]
-        return [
-            remote(block, block, x_s.at[p, 1], x_r.at[p, 1], partner),
-            remote(block, block, x_s.at[p, 2], x_r.at[p, 2], sibling),
-        ]
+        remote(block, block, x_s.at[p], x_r.at[p, 2], sibling)
+        return remote(block, block, x_s.at[p], x_r.at[p, 1], partner)
 
     def pass_last(p, passed):
         k, off, w = PIECES[p]
-        passed[0].wait_recv()
+        passed.wait_recv()
         block = results[k].at[:, at128(half + other * QUART + off, w)]
-        passed.append(remote(block, block, x_s.at[p, 3], x_r.at[p, 3], sibling))
-
-    shifts = []
-    for p in range(2):
+        remote(block, block, x_s.at[p], x_r.at[p, 2], sibling)
+
+    def forward_result(p):
         k, off, w = PIECES[p]
-        shifts.append(
-            ship(p, hid[:, at128(quarter + off, w)].astype(F32) + combine(p), after)
-        )
-    backs.append(give_back(2, pairs[2]))
+        return hid[:, at128(quarter + off, w)].astype(F32) + combine(p)
+
+    shifts = [ship(0, forward_result(0), after)]
+    shifts.append(ship(1, forward_result(1), after))
     passed = [pass_on(0, shifts[0])]
-    backs.append(give_back(3, pairs[3]))
+    give_back(2, pairs[2])
     passed.append(pass_on(1, shifts[1]))
-
-    for copy in notes:
-        copy.wait_recv()
+    give_back(3, pairs[3])
+
+    take(scr.at[0:120, :], c_r.at[0])
     lane_at = (me % 8) * 16
     row, col = iota((128, ROWS), 0), iota((128, ROWS), 1)
     turn = jnp.where(row == lane_at + (col & 15), 1.0, 0.0)
@@ -540,11 +530,20 @@
     passed.append(pass_on(3, shifts[3]))
     pass_last(2, passed[2])
     pass_last(3, passed[3])
-    for copies in passed:
-        copies[1].wait_recv()
-        copies[2].wait_recv()
-    for copy in everything:
-        copy.wait_send()
+    for p in range(COUNT):
+        take(bufs[p][10], x_r.at[p, 2])
+    for k in range(2):
+        take(send.at[k, 0:144, :], d_s.at[k])
+        take(send.at[k, 0:96, :], f_s.at[k])
+        take(send.at[k], s_s.at[k])
+    for p in range(COUNT):
+        es, cp, ret = bufs[p][0], bufs[p][3], bufs[p][10]
+        take(es, e_s.at[p])
+        take(cp.at[0:128, :], p_s.at[p])
+        take(ret.at[0:240, :], r_s.at[p])
+        take(es, x_s.at[p])
+    take(sc.at[0:3], a_s.at[0])
+    take(scr.at[0:120, :], c_s.at[0])
 
 
 def shards(tokens, cotangent, gain, router, w_gate, w_up, w_down, expert_ids):
@@ -558,6 +557,9 @@
         return pltpu.SemaphoreType.DMA(shape)
 
     scratch = [
+        buf(2, 2, TOK // 2, dtype=jnp.int32),
+        buf(1, D, dtype=F32),
+        buf(16, D),
         buf(TOK, D),
         buf(TOK, D),
         buf(TOK, D),
@@ -581,25 +583,25 @@
         buf(4, 8, ROWS, dtype=F32),
         buf(8, ROWS, dtype=F32),
         buf(128, 128, dtype=F32),
-        sems(5),
-        sems(2, 11),
-        sems(2, 11),
-        sems(2, 8),
-        sems(2, 8),
-        sems(2, 4),
-        sems(2, 4),
+        sems(8),
+        sems(2),
+        sems(2, 9),
+        sems(2),
+        sems(2, 2),
+        sems(2),
+        sems(2),
+        sems(COUNT),
         sems(COUNT),
         sems(COUNT),
         sems(COUNT, 3),
+        sems(COUNT),
+        sems(COUNT),
+        sems(1),
+        sems(1),
+        sems(1),
+        sems(1),
+        sems(COUNT),
         sems(COUNT, 3),
-        sems(COUNT, 15),
-        sems(COUNT, 15),
-        sems(3),
-        sems(3),
-        sems(15),
-        sems(15),
-        sems(COUNT, 4),
-        sems(COUNT, 4),
     ]
     for _, _, w in PIECES:
         scratch += [
@@ -620,7 +622,7 @@
     section_out, section_grad = pl.pallas_call(
         kernel,
         out_shape=(out, out),
-        in_specs=[anywhere, anywhere, vmem, vmem, anywhere, anywhere, anywhere, vmem],
+        in_specs=[anywhere] * 8,
         out_specs=(vmem, vmem),
         scratch_shapes=scratch,
         compiler_params=pltpu.CompilerParams(

time: 87.5 us -> 84.6 us (0.967)
  Pallas kernels: 84.9 us -> 82 us
    pallas_call x1, Pallas kernels: 84.9 us -> 82 us  [shards(): pl.pallas_call(kernel, out_shape=(out, out), in_specs=[anywhere] * 8, out...]
where the time goes in v2:
time: 84.6 us; the launch traced here: 84.5 us
  Pallas kernels  82 us (97%)
  local copies, waits for them, and re-layouts  1.85 us (2%)
    pallas_call x1, Pallas kernels, shards(): pl.pallas_call(kernel, out_shape=(out, out), in_specs=[anywhere] * 8, out...  82 us
    unnamed x2, local copies, waits for them, and re-layouts  1.85 us

profile of v2, /device:TPU:1, one launch (start us, length us, event | category | flops | bytes accessed | tf_op | source)
XLA Modules:
  0.0 84.5 jit_solution(3759016282830711105)
XLA Ops:
  0.6 82.0 %shard_map.95 = (bf16[128,3584]{1,0:T(8,128)(2,1)S(1)}, bf16[128,3584]{1,0:T(8,128)(2,1)S(1)}) custom-call(bf16[128,3584]{1,0:T(8,128)(2,1)} %bitcast.18, bf16[128,3584]{1,0:T(8,128)(2,1)} %bitcast.19, f32[1,3584]{1,0:T(1,128)} %gain_h.1, bf16[16,3584]{1,0:T(8,128)(2,1)} %bitcast.20, bf16[3584,256]{1,0:T(8,128)(2,1)} %bitcast.15, ...), custom_call_target="tpu_custom_call" | custom-call | tf_op jit(solution)/shard_map/pallas_call | solution.py:622
  82.6 0.9 %copy.12 = bf16[1,2,64,3584]{3,2,1,0:T(8,128)(2,1)} copy(bf16[1,2,64,3584]{3,2,1,0:T(8,128)(2,1)S(1)} %bitcast.14) | data formatting | bytes 1835008
  83.5 0.9 %copy.13 = bf16[1,2,64,3584]{3,2,1,0:T(8,128)(2,1)} copy(bf16[1,2,64,3584]{3,2,1,0:T(8,128)(2,1)S(1)} %bitcast.13) | data formatting | bytes 1835008

commit v3 on v2

--- a/solution.py
+++ b/solution.py
@@ -19,7 +19,7 @@
 ROWS = 256
 HALF = D // 2
 QUART = D // 4
-PIECES = ((0, 0, 512), (0, 512, 384), (1, 0, 512), (1, 512, 384))
+PIECES = ((0, 0, 512), (0, 512, 384), (1, 0, 640), (1, 640, 256))
 COUNT = len(PIECES)
 
 
@@ -420,6 +420,7 @@
     gg[...] = (a * u * sigma * (1.0 + g * (1.0 - sigma))).astype(BF16)
     ug[...] = (a * g * sigma).astype(BF16)
     swaps += [swap(2), swap(3)]
+    give_back(0, pairs[0])
 
     ones = jnp.ones((8, HID), F32)
     w_row = dot_nt(ones, act[...].astype(F32) * act_g[...], HIGHEST)
@@ -431,7 +432,6 @@
     for device in (sibling, partner, diagonal):
         remote(sc.at[dx], sc.at[dx], a_s.at[0], a_r.at[0], device)
     keep(2)
-    give_back(0, pairs[0])
     pairs.append(pair_sum(2, swaps[2]))
     keep(3)
     give_back(1, pairs[1])

time: 84.6 us -> 83.7 us (0.989)
  Pallas kernels: 82 us -> 81.1 us
    pallas_call x1, Pallas kernels: 82 us -> 81.1 us  [shards(): pl.pallas_call(kernel, out_shape=(out, out), in_specs=[anywhere] * 8, out...]
where the time goes in v3:
time: 83.7 us; the launch traced here: 83.6 us
  Pallas kernels  81.1 us (97%)
  local copies, waits for them, and re-layouts  1.85 us (2%)
    pallas_call x1, Pallas kernels, shards(): pl.pallas_call(kernel, out_shape=(out, out), in_specs=[anywhere] * 8, out...  81.1 us
    unnamed x2, local copies, waits for them, and re-layouts  1.85 us

profile of v3, /device:TPU:1, one launch (start us, length us, event | category | flops | bytes accessed | tf_op | source)
XLA Modules:
  0.0 83.6 jit_solution(2777320060945338630)
XLA Ops:
  0.6 81.1 %shard_map.95 = (bf16[128,3584]{1,0:T(8,128)(2,1)S(1)}, bf16[128,3584]{1,0:T(8,128)(2,1)S(1)}) custom-call(bf16[128,3584]{1,0:T(8,128)(2,1)} %bitcast.18, bf16[128,3584]{1,0:T(8,128)(2,1)} %bitcast.19, f32[1,3584]{1,0:T(1,128)} %gain_h.1, bf16[16,3584]{1,0:T(8,128)(2,1)} %bitcast.20, bf16[3584,256]{1,0:T(8,128)(2,1)} %bitcast.15, ...), custom_call_target="tpu_custom_call" | custom-call | tf_op jit(solution)/shard_map/pallas_call | solution.py:622
  81.8 0.9 %copy.12 = bf16[1,2,64,3584]{3,2,1,0:T(8,128)(2,1)} copy(bf16[1,2,64,3584]{3,2,1,0:T(8,128)(2,1)S(1)} %bitcast.14) | data formatting | bytes 1835008
  82.7 0.9 %copy.13 = bf16[1,2,64,3584]{3,2,1,0:T(8,128)(2,1)} copy(bf16[1,2,64,3584]{3,2,1,0:T(8,128)(2,1)S(1)} %bitcast.13) | data formatting | bytes 1835008

commit v4 on v3

--- a/solution.py
+++ b/solution.py
@@ -420,8 +420,6 @@
     gg[...] = (a * u * sigma * (1.0 + g * (1.0 - sigma))).astype(BF16)
     ug[...] = (a * g * sigma).astype(BF16)
     swaps += [swap(2), swap(3)]
-    give_back(0, pairs[0])
-
     ones = jnp.ones((8, HID), F32)
     w_row = dot_nt(ones, act[...].astype(F32) * act_g[...], HIGHEST)
     n_row = dot_nt(
@@ -431,12 +429,49 @@
     sc[dx] = jnp.where(line == 0, w_row, jnp.where(line == 1, n_row, 0.0))
     for device in (sibling, partner, diagonal):
         remote(sc.at[dx], sc.at[dx], a_s.at[0], a_r.at[0], device)
+    give_back(0, pairs[0])
+
     keep(2)
     pairs.append(pair_sum(2, swaps[2]))
     keep(3)
     give_back(1, pairs[1])
     pairs.append(pair_sum(3, swaps[3]))
 
+    quarter = half + zl * QUART
+    results = (out_v, grad_v)
+
+    def combine(p):
+        ret = bufs[p][10]
+        take(ret.at[0:240, :], r_r.at[p])
+        return dot(cwh[...], ret[...]) + dot(cwl[...], ret[...])
+
+    def ship(p, value, device):
+        k, off, w = PIECES[p]
+        fin = bufs[p][11]
+        fin[...] = value.astype(BF16)
+        return remote(
+            fin, results[k].at[:, at128(quarter + off, w)], x_s.at[p], x_r.at[p, 0], device
+        )
+
+    def pass_on(p, shift):
+        k, off, w = PIECES[p]
+        shift.wait_recv()
+        block = results[k].at[:, at128(quarter + off, w)]
+        remote(block, block, x_s.at[p], x_r.at[p, 2], sibling)
+        return remote(block, block, x_s.at[p], x_r.at[p, 1], partner)
+
+    def pass_last(p, passed):
+        k, off, w = PIECES[p]
+        passed.wait_recv()
+        block = results[k].at[:, at128(half + other * QUART + off, w)]
+        remote(block, block, x_s.at[p], x_r.at[p, 2], sibling)
+
+    def forward_result(p):
+        k, off, w = PIECES[p]
+        return hid[:, at128(quarter + off, w)].astype(F32) + combine(p)
+
+    shifts = [ship(0, forward_result(0), after)]
+    shifts.append(ship(1, forward_result(1), after))
     take(sc.at[0:3], a_r.at[0])
     scs[...] = (sc[0] + sc[1]) + (sc[2] + sc[3])
     own_notes = at8(me * 8, 8)
@@ -451,41 +486,6 @@
             )
     scr[own_notes, :] = scs[:, at128((zh // 2) * 128, 128)]
 
-    quarter = half + zl * QUART
-    results = (out_v, grad_v)
-
-    def combine(p):
-        ret = bufs[p][10]
-        take(ret.at[0:240, :], r_r.at[p])
-        return dot(cwh[...], ret[...]) + dot(cwl[...], ret[...])
-
-    def ship(p, value, device):
-        k, off, w = PIECES[p]
-        fin = bufs[p][11]
-        fin[...] = value.astype(BF16)
-        return remote(
-            fin, results[k].at[:, at128(quarter + off, w)], x_s.at[p], x_r.at[p, 0], device
-        )
-
-    def pass_on(p, shift):
-        k, off, w = PIECES[p]
-        shift.wait_recv()
-        block = results[k].at[:, at128(quarter + off, w)]
-        remote(block, block, x_s.at[p], x_r.at[p, 2], sibling)
-        return remote(block, block, x_s.at[p], x_r.at[p, 1], partner)
-
-    def pass_last(p, passed):
-        k, off, w = PIECES[p]
-        passed.wait_recv()
-        block = results[k].at[:, at128(half + other * QUART + off, w)]
-        remote(block, block, x_s.at[p], x_r.at[p, 2], sibling)
-
-    def forward_result(p):
-        k, off, w = PIECES[p]
-        return hid[:, at128(quarter + off, w)].astype(F32) + combine(p)
-
-    shifts = [ship(0, forward_result(0), after)]
-    shifts.append(ship(1, forward_result(1), after))
     passed = [pass_on(0, shifts[0])]
     give_back(2, pairs[2])
     passed.append(pass_on(1, shifts[1]))

time: 83.7 us -> 83.7 us (level)
  no operation moved by 1% of the time
where the time goes in v4:
time: 83.7 us; the launch traced here: 83.6 us
  Pallas kernels  81.1 us (97%)
  local copies, waits for them, and re-layouts  1.85 us (2%)
    pallas_call x1, Pallas kernels, shards(): pl.pallas_call(kernel, out_shape=(out, out), in_specs=[anywhere] * 8, out...  81.1 us
    unnamed x2, local copies, waits for them, and re-layouts  1.85 us

profile of v4, /device:TPU:1, one launch (start us, length us, event | category | flops | bytes accessed | tf_op | source)
XLA Modules:
  0.0 83.6 jit_solution(8053824935149657584)
XLA Ops:
  0.6 81.1 %shard_map.95 = (bf16[128,3584]{1,0:T(8,128)(2,1)S(1)}, bf16[128,3584]{1,0:T(8,128)(2,1)S(1)}) custom-call(bf16[128,3584]{1,0:T(8,128)(2,1)} %bitcast.18, bf16[128,3584]{1,0:T(8,128)(2,1)} %bitcast.19, f32[1,3584]{1,0:T(1,128)} %gain_h.1, bf16[16,3584]{1,0:T(8,128)(2,1)} %bitcast.20, bf16[3584,256]{1,0:T(8,128)(2,1)} %bitcast.15, ...), custom_call_target="tpu_custom_call" | custom-call | tf_op jit(solution)/shard_map/pallas_call | solution.py:622
  81.7 0.9 %copy.12 = bf16[1,2,64,3584]{3,2,1,0:T(8,128)(2,1)} copy(bf16[1,2,64,3584]{3,2,1,0:T(8,128)(2,1)S(1)} %bitcast.14) | data formatting | bytes 1835008
  82.7 0.9 %copy.13 = bf16[1,2,64,3584]{3,2,1,0:T(8,128)(2,1)} copy(bf16[1,2,64,3584]{3,2,1,0:T(8,128)(2,1)S(1)} %bitcast.13) | data formatting | bytes 1835008
